TPU v7x, 32 devices: a whole 2x2x4 slice. The times are simulated.
32 devices in a mesh: groups: 2 (over y), expert: 4 (over x, core), mp: 4 (over z).
Axes of the slice: x: 2, y: 2, z: 4, core: 2. Of those that a mesh axis runs over, the one named last changes fastest.
Arguments:
- output_gradient: bfloat16 [2048, 6144], P(('groups', 'expert'), 'mp'), parts along dimension 0, may hold values from -1.5 to 1.5
- routes: int32 [2048, 2], P(('groups', 'expert')), parts along dimension 0, may hold values from 0 to 3, all different within a row; in each aligned block of 256 rows (0 to 255, 256 to 511, ...) at most 128 rows name the same one
- mixture_coefficients: bfloat16 [2048, 2], P(('groups', 'expert')), parts along dimension 0, may hold values from 0.099609375 to 0.8984375
- gate_preactivation: bfloat16 [4, 1024, 8192], P('expert', 'groups', 'mp'), parts along dimension 1, may hold values from -6 to 6
- up_projection_saved: bfloat16 [4, 1024, 8192], P('expert', 'groups', 'mp'), parts along dimension 1, may hold values from -6 to 6
- down_matrix: bfloat16 [4, 8192, 6144], P('expert', 'mp'), may hold values from -0.0625 to 0.0625
- lowrank_left_matrix: bfloat16 [4, 16, 8192], P('expert', None, 'mp'), may hold values from -0.0625 to 0.0625
- lowrank_right_matrix: bfloat16 [4, 16, 6144], P('expert'), may hold values from -0.078125 to 0.078125
Outputs:
- gate_grad: bfloat16 [4, 1024, 8192], P('expert', 'groups', 'mp'), parts along dimension 1
- up_grad: bfloat16 [4, 1024, 8192], P('expert', 'groups', 'mp'), parts along dimension 1
- lora_a_grad: float32 [8, 16, 8192], P(('groups', 'expert'), None, 'mp'), parts along dimension 0
- lora_b_grad: float32 [8, 16, 6144], P(('groups', 'expert'), None, 'mp'), parts along dimension 0
- weight_grad: float32 [2048, 2], P(('groups', 'expert')), parts along dimension 0
There are 2 independent parts, one for each index of `groups`. A program takes and returns all parts, laid end to end along the dimension named above; an argument that names none is the same for every part. Nothing has to cross between parts.
Inputs may be any that keep to these rules, and one draw needn't show every extreme that they name: `routes`: each token names 2 different experts; the rows of one owner name no expert more than 128 times, a bound that some block reaches.
All inputs are finite; a program needn't handle non-finite values.
Results may differ from a plain program's by a relative error of at most 0.005.
Values may be sent and summed in bfloat16 or wider, within the bound.
A program may use at most 128 MiB of HBM per device.

v0:
```python
import jax
import jax.numpy as jnp
from jax import lax
from jax.sharding import PartitionSpec as P

CAP = 128


adapter_scale = 2.0


def positions(flat, count):
    hot = (flat[:, None] == jnp.arange(count, dtype=jnp.int32)[None, :]).astype(jnp.int32)
    before = jnp.cumsum(hot, axis=0) - hot
    return jnp.sum(before * hot, axis=1)


def contract_last(left, right):
    return lax.dot_general(
        left, right, (((1,), (1,)), ((), ())), preferred_element_type=jnp.float32
    )


def body(
    output_gradient,
    routes,
    mixture_coefficients,
    gate_preactivation,
    up_projection_saved,
    down_matrix,
    lowrank_left_matrix,
    lowrank_right_matrix,
):
    experts = lax.axis_size("expert")
    tok_rows = output_gradient.shape[0]
    slice_width = output_gradient.shape[1]
    flat = routes.reshape(-1)
    place = positions(flat, experts)
    owner_pick = (
        jnp.zeros((experts, CAP), jnp.bfloat16)
        .at[flat, place]
        .set(mixture_coefficients.reshape(-1))
    )
    weight_local = down_matrix[0]
    second_factor_shard = lowrank_right_matrix[0]
    first_factor_shard = lowrank_left_matrix[0]
    repeated = jnp.repeat(output_gradient, 2, axis=0)
    buffer = jnp.zeros((experts, CAP, slice_width), jnp.bfloat16).at[flat, place].set(repeated)
    got_rows, got_pick = (
        lax.all_to_all(buffer, "expert", split_axis=0, concat_axis=0, tiled=True),
        lax.all_to_all(owner_pick, "expert", split_axis=0, concat_axis=0, tiled=True),
    )
    slice_rows = got_rows.reshape(experts * CAP, slice_width)
    selected_slots = got_pick.reshape(-1)
    piece = lax.all_gather(slice_rows, "mp", axis=1, tiled=True)
    base_gradient = contract_last(piece, weight_local)
    back32 = contract_last(piece, second_factor_shard)
    gate32 = gate_preactivation[0].astype(jnp.float32)
    up32 = up_projection_saved[0].astype(jnp.float32)
    sigma = jax.nn.sigmoid(gate32)
    act = gate32 * sigma
    hidden = (act * up32).astype(jnp.bfloat16)
    low_part = contract_last(hidden, first_factor_shard)
    backward_result = back32.astype(jnp.bfloat16)
    hidden_gradient = base_gradient + adapter_scale * jnp.dot(
        backward_result, first_factor_shard, preferred_element_type=jnp.float32
    )
    hidden_float = hidden.astype(jnp.float32)
    score_part = jnp.sum(hidden_float * hidden_gradient, axis=1)
    rank_projection, score = lax.psum((low_part, score_part), "mp")
    scaling_factor = selected_slots.astype(jnp.float32)[:, None]
    scaled = scaling_factor * hidden_gradient
    gate_grad = (scaled * up32 * sigma * (1.0 + gate32 * (1.0 - sigma))).astype(jnp.bfloat16)
    up_grad = (scaled * act).astype(jnp.bfloat16)
    first_factor_gradient = adapter_scale * jnp.dot(
        (scaling_factor * backward_result.astype(jnp.float32)).T,
        hidden_float,
        precision=lax.Precision.HIGHEST,
    )
    second_factor_gradient = adapter_scale * jnp.dot(
        (scaling_factor * rank_projection).T,
        slice_rows.astype(jnp.float32),
        precision=lax.Precision.HIGHEST,
    )
    returned = lax.all_to_all(
        score.reshape(experts, CAP), "expert", split_axis=0, concat_axis=0, tiled=True
    )
    weight_grad = returned[flat, place].reshape(tok_rows, 2)
    return (
        gate_grad[None],
        up_grad[None],
        first_factor_gradient[None],
        second_factor_gradient[None],
        weight_grad,
    )


def solution(mesh):
    placed = (
        P(("groups", "expert"), "mp"),
        P(("groups", "expert"), None),
        P(("groups", "expert"), None),
        P("expert", "groups", "mp"),
        P("expert", "groups", "mp"),
        P("expert", "mp", None),
        P("expert", None, "mp"),
        P("expert", None, None),
    )
    return jax.shard_map(
        body,
        mesh=mesh,
        in_specs=placed,
        out_specs=(
            P("expert", "groups", "mp"),
            P("expert", "groups", "mp"),
            P(("groups", "expert"), None, "mp"),
            P(("groups", "expert"), None, "mp"),
            P(("groups", "expert"), None),
        ),
        check_vma=False,
    )
```

profile of v0, /device:TPU:0, one launch (start us, length us, event | category | flops | bytes accessed | tf_op | source)
XLA Modules:
  0.0 263.7 jit_solution(16780571639160607792)
XLA Ops:
  7.2 0.0 copy-start
  7.2 0.0 all-gather.2.cloned.1.call-start
  7.2 0.8 copy.18
  8.1 0.1 eq.29
  8.2 0.1 eq.25
  8.4 0.1 reshape.103
  8.5 1.2 reduce-window.6
  9.8 0.2 slice_reduce_fusion
  10.0 0.2 reduce-window.9
  10.1 0.1 add_bitcast_fusion
  10.2 2.0 broadcast_in_dim.31
  12.2 0.6 reshape.126
  12.9 0.1 broadcast_in_dim.30
  13.0 39.5 %scatter_fusion.1 = bf16[4,128,1536]{2,1,0:T(8,128)(2,1)S(1)} fusion(bf16[4,128,1536]{2,1,0:T(8,128)(2,1)S(1)} %broadcast_in_dim.30, s32[512]{0:T(512)S(1)} %bitcast.104, bf16[512,1536]{1,0:T(8,128)(2,1)S(1)} %reshape.126), kind=kCustom, calls=%fused_computation.2 | custom fusion | bytes 4722688 | tf_op jit(solution)/shard_map/scatter | solution.py:48
  52.5 0.0 copy-start.2
  52.5 0.0 copy-start.3
  52.5 24.3 %all_to_all.26 = bf16[4,128,1536]{2,1,0:T(8,128)(2,1)} all-to-all(bf16[4,128,1536]{2,1,0:T(8,128)(2,1)S(1)} %scatter_fusion.1), channel_id=1, replica_groups=mesh['groups'=2,'expert'=4,'mp'=4] {'expert'}, dimensions={0} | all-to-all | bytes 3145728 | tf_op jit(solution)/shard_map/all_to_all | solution.py:50
  76.9 0.0 all-gather.2.cloned.1.call-update
  76.9 0.0 copy-done.2
  76.9 0.1 copy.21
  77.0 0.1 reshape.120
  77.2 22.9 %scatter_fusion = bf16[4,128]{1,0:T(4,128)(2,1)S(1)} fusion(bf16[4,128]{1,0:T(4,128)(2,1)S(1)} %broadcast_in_dim.14, s32[512]{0:T(512)S(1)} %bitcast.105, bf16[512]{0:T(512)(128)(2,1)S(1)} %reshape.120), kind=kCustom, calls=%fused_computation.1 | custom fusion | bytes 7168 | tf_op jit(solution)/shard_map/scatter | solution.py:42
  100.2 0.6 copy.22
  100.7 3.4 %all-to-all-start = ((bf16[4,1,128]{2,1,0:T(2,128)(2,1)}), bf16[4,1,128]{2,1,0:T(2,128)(2,1)S(1)}, u32[]{:S(2)}, u32[]{:S(2)}) async-start(bf16[4,1,128]{2,1,0:T(2,128)(2,1)} %copy.22), calls=%async_computation | async-start | bytes 4096 | tf_op jit(solution)/shard_map/all_to_all | solution.py:51
  104.1 0.0 copy-done.3
  104.2 3.6 %fusion.22 = f32[512,16]{0,1:T(8,128)S(1)} fusion(bf16[1,512,2048]{2,1,0:T(8,128)(2,1)} %param.12, bf16[1,512,2048]{2,1,0:T(8,128)(2,1)} %param.11, bf16[1,16,2048]{2,1,0:T(8,128)(2,1)S(1)} %copy-done.3), kind=kOutput, calls=%fused_computation.35 | convolution fusion | flops 41943040 | bytes 4292608 | tf_op jit(solution)/shard_map/dot_general | solution.py:19
  107.7 0.0 all-to-all-done
  107.7 85.5 %all-gather.2.cloned.1.call-done = bf16[512,6144]{1,0:T(8,128)(2,1)} async-done(((bf16[512,1536]{1,0:T(8,128)(2,1)}), bf16[512,6144]{1,0:T(8,128)(2,1)}) %all-gather.2.cloned.1.call-update) | async-done | bytes 6291472 | tf_op jit(solution)/shard_map/all_gather | solution.py:55
  193.3 0.0 copy-done
  193.3 4.5 %convolution_convert_fusion = bf16[512,16]{0,1:T(8,128)(2,1)S(1)} fusion(bf16[512,6144]{1,0:T(8,128)(2,1)} %all-gather.2.cloned.1.call-done, bf16[1,16,6144]{2,1,0:T(8,128)(2,1)S(1)} %copy-done), kind=kOutput, calls=%fused_computation.38 | convolution fusion | flops 100671488 | bytes 6504448 | tf_op jit(solution)/shard_map/dot_general | solution.py:19
  197.8 21.1 %fusion = f32[512,2048]{1,0:T(8,128)} fusion(bf16[512,6144]{1,0:T(8,128)(2,1)} %all-gather.2.cloned.1.call-done, bf16[1,2048,6144]{2,1,0:T(8,128)(2,1)} %param.13), kind=kOutput, calls=%fused_computation.3 | convolution fusion | flops 12884901888 | bytes 35651584 | tf_op jit(solution)/shard_map/dot_general | solution.py:19
  218.9 0.0 copy-start.1
  218.9 7.0 %multiply_reduce_fusion = (f32[512]{0:T(512)S(1)}, bf16[512,2048]{1,0:T(8,128)(2,1)S(1)}, bf16[1,512,2048]{2,1,0:T(8,128)(2,1)}, bf16[1,512,2048]{2,1,0:T(8,128)(2,1)}) fusion(bf16[1,512,2048]{2,1,0:T(8,128)(2,1)} %param.12, bf16[1,512,2048]{2,1,0:T(8,128)(2,1)} %param.11, f32[512]{0:T(512)S(1)} %bitcast.109, f32[512,2048]{1,0:T(8,128)} %fusion, ...), kind=kOutput, calls=%fused_computation.27 | convolution fusion | flops 57671168 | bytes 14766080 | tf_op jit(solution)/shard_map/dot_general | solution.py:65
  225.9 1.6 fusion.20
  227.5 17.0 %all-reduce = (f32[512,16]{0,1:T(8,128)S(1)}, f32[4,1,128]{2,1,0:T(1,128)}) all-reduce(f32[512,16]{0,1:T(8,128)S(1)} %fusion.22, f32[4,1,128]{2,1,0:T(1,128)S(1)} %bitcast.114), channel_id=1, replica_groups=mesh['groups'=2,'expert'=4,'mp'=4] {'mp'}, use_global_device_ids=true, to_apply=%region_5.6 | all-reduce | flops 8704 | bytes 69632 | tf_op jit(solution)/shard_map/psum | solution.py:70
  244.5 3.2 %all-to-all-start.2 = ((f32[4,1,128]{2,1,0:T(1,128)}), f32[4,1,128]{2,1,0:T(1,128)S(1)}, u32[]{:S(2)}, u32[]{:S(2)}) async-start(f32[4,1,128]{2,1,0:T(1,128)} %get-tuple-element.16), calls=%async_computation.2 | async-start | bytes 4096 | tf_op jit(solution)/shard_map/all_to_all | solution.py:85
  247.7 0.0 copy-done.1
  247.8 1.4 fusion.19
  249.1 2.3 all-to-all-done.2
  251.4 4.7 %gather_fusion = f32[512]{0:T(512)S(1)} fusion(f32[4,128]{1,0:T(4,128)S(1)} %bitcast.102, s32[512]{0:T(512)S(1)} %bitcast.106), kind=kCustom, calls=%fused_computation | custom fusion | bytes 8192 | tf_op jit(solution)/shard_map/gather | solution.py:88
  256.1 0.1 reshape.108
  256.2 0.7 copy.23
  (5 shorter events, 0.1 us)
Async XLA Ops:
  7.2 186.1 %copy-start = (bf16[1,16,6144]{2,1,0:T(8,128)(2,1)S(1)}, bf16[1,16,6144]{2,1,0:T(8,128)(2,1)}, u32[]{:S(2)}) copy-start(bf16[1,16,6144]{2,1,0:T(8,128)(2,1)} %param.15) | copy-start | bytes 589828
  7.2 186.1 %all-gather.2.cloned.1.call-start = ((), (), s32[]{:S(2)}) async-start(), calls=%async_computation.3 | async-start | bytes 7864320 | tf_op jit(solution)/shard_map/all_gather | solution.py:55
  52.5 24.4 %copy-start.2 = (bf16[256,2]{0,1:T(2,128)(2,1)S(1)}, bf16[256,2]{0,1:T(2,128)(2,1)}, u32[]{:S(2)}) copy-start(bf16[256,2]{0,1:T(2,128)(2,1)} %param.10) | copy-start | bytes 3076
  52.5 51.6 %copy-start.3 = (bf16[1,16,2048]{2,1,0:T(8,128)(2,1)S(1)}, bf16[1,16,2048]{2,1,0:T(8,128)(2,1)}, u32[]{:S(2)}) copy-start(bf16[1,16,2048]{2,1,0:T(8,128)(2,1)} %param.14) | copy-start | bytes 196612
  100.7 7.0 %all-to-all-start = ((bf16[4,1,128]{2,1,0:T(2,128)(2,1)}), bf16[4,1,128]{2,1,0:T(2,128)(2,1)S(1)}, u32[]{:S(2)}, u32[]{:S(2)}) async-start(bf16[4,1,128]{2,1,0:T(2,128)(2,1)} %copy.22), calls=%async_computation | async-start | bytes 4096 | tf_op jit(solution)/shard_map/all_to_all | solution.py:51
  218.9 28.9 %copy-start.1 = (bf16[4,128,1536]{2,1,0:T(8,128)(2,1)S(1)}, bf16[4,128,1536]{2,1,0:T(8,128)(2,1)}, u32[]{:S(2)}) copy-start(bf16[4,128,1536]{2,1,0:T(8,128)(2,1)} %all_to_all.26) | copy-start | bytes 4718596
  244.5 6.9 %all-to-all-start.2 = ((f32[4,1,128]{2,1,0:T(1,128)}), f32[4,1,128]{2,1,0:T(1,128)S(1)}, u32[]{:S(2)}, u32[]{:S(2)}) async-start(f32[4,1,128]{2,1,0:T(1,128)} %get-tuple-element.16), calls=%async_computation.2 | async-start | bytes 4096 | tf_op jit(solution)/shard_map/all_to_all | solution.py:85
Sparse Core Ops, SparseCore 0:
  77.0 116.2 all-gather.1
where the time goes:
time: 264 us
  waiting for transfers between devices  87.8 us (33%)
  local copies, waits for them, and re-layouts  73 us (28%)
  blocking collectives  41.4 us (16%)
  matrix products  39.1 us (15%)
  between operations  14.2 us (5%)
  starting transfers between devices  6.66 us (3%)
    all_gather x1, waiting for transfers between devices, body(): piece = lax.all_gather(slice_rows, 'mp', axis=1, tiled=True)  85.5 us
    scatter x1, local copies, waits for them, and re-layouts, body(): jnp.zeros((experts, CAP, slice_width), jnp.bfloat16).at[flat, place]  39.5 us
    dot_general x3, matrix products, contract_last(): lax.dot_general(left, right, (((1,), (1,)), ((), ())), preferred_element_...  29.2 us
    all_to_all x1, blocking collectives, body(): lax.all_to_all(buffer, 'expert', split_axis=0, concat_axis=0, tiled=True)  24.3 us
    scatter x1, local copies, waits for them, and re-layouts, body(): owner_pick = jnp.zeros((experts, CAP), jnp.bfloat16).at[flat, place].set(...  22.9 us
    psum x1, blocking collectives, body(): rank_projection, score = lax.psum((low_part, score_part), 'mp')  17 us
    dot_general x1, matrix products, body(): jnp.dot(backward_result, first_factor_shard, preferred_element_type=jnp.f...  7 us
  transfers between devices with their start and end apart: 3, of which 2 were waited for; matrix products, arithmetic and copies ran while one was open for 11% of the time, Pallas kernels for 0%

commit v1 on v0

--- a/solution.py
+++ b/solution.py
@@ -36,16 +36,27 @@
     slice_width = output_gradient.shape[1]
     flat = routes.reshape(-1)
     place = positions(flat, experts)
+    key = (flat * CAP + place).reshape(tok_rows, 2)
+    slots = jnp.arange(experts * CAP, dtype=jnp.int32)
+    first = slots[:, None] == key[None, :, 0]
+    second = slots[:, None] == key[None, :, 1]
+    mix32 = mixture_coefficients.astype(jnp.float32)
     owner_pick = (
-        jnp.zeros((experts, CAP), jnp.bfloat16)
-        .at[flat, place]
-        .set(mixture_coefficients.reshape(-1))
+        jnp.sum(
+            jnp.where(first, mix32[None, :, 0], 0.0) + jnp.where(second, mix32[None, :, 1], 0.0),
+            axis=1,
+        )
+        .astype(jnp.bfloat16)
+        .reshape(experts, CAP)
     )
     weight_local = down_matrix[0]
     second_factor_shard = lowrank_right_matrix[0]
     first_factor_shard = lowrank_left_matrix[0]
-    repeated = jnp.repeat(output_gradient, 2, axis=0)
-    buffer = jnp.zeros((experts, CAP, slice_width), jnp.bfloat16).at[flat, place].set(repeated)
+    buffer = jnp.dot(
+        (first | second).astype(jnp.bfloat16),
+        output_gradient,
+        preferred_element_type=jnp.float32,
+    ).astype(jnp.bfloat16).reshape(experts, CAP, slice_width)
     got_rows, got_pick = (
         lax.all_to_all(buffer, "expert", split_axis=0, concat_axis=0, tiled=True),
         lax.all_to_all(owner_pick, "expert", split_axis=0, concat_axis=0, tiled=True),
@@ -85,7 +96,14 @@
     returned = lax.all_to_all(
         score.reshape(experts, CAP), "expert", split_axis=0, concat_axis=0, tiled=True
     )
-    weight_grad = returned[flat, place].reshape(tok_rows, 2)
+    returned_flat = returned.reshape(1, -1)
+    weight_grad = jnp.stack(
+        [
+            jnp.sum(jnp.where(key[:, k : k + 1] == slots[None, :], returned_flat, 0.0), axis=1)
+            for k in range(2)
+        ],
+        axis=1,
+    )
     return (
         gate_grad[None],
         up_grad[None],

time: 264 us -> 218 us (0.83)
  local copies, waits for them, and re-layouts: 73 us -> 2.21 us
  waiting for transfers between devices: 87.8 us -> 109 us
    scatter x2 -> x0, local copies, waits for them, and re-layouts: 62.5 us -> none  [the longest x1 39.5 us: body(): jnp.zeros((experts, CAP, slice_width), jnp.bfloat16).at[flat, place]]
    all_gather x1, waiting for transfers between devices: 85.5 us -> 109 us  [body(): piece = lax.all_gather(slice_rows, 'mp', axis=1, tiled=True)]
    gather x1 -> x0, local copies, waits for them, and re-layouts: 4.66 us -> none  [body(): weight_grad = returned[flat, place].reshape(tok_rows, 2)]
  transfers between devices with their start and end apart: 3 -> 3, of which waited for: 2 -> 1; matrix products, arithmetic and copies ran while one was open for 11% -> 4% of each run, Pallas kernels for 0% -> 0%
where the time goes in v1:
time: 218 us
  waiting for transfers between devices  109 us (50%)
  matrix products  41.7 us (19%)
  blocking collectives  41.2 us (19%)
  between operations  14.1 us (6%)
  starting transfers between devices  6.48 us (3%)
  other arithmetic  3.25 us (1%)
  local copies, waits for them, and re-layouts  2.21 us (1%)
    all_gather x1, waiting for transfers between devices, body(): piece = lax.all_gather(slice_rows, 'mp', axis=1, tiled=True)  109 us
    dot_general x3, matrix products, contract_last(): lax.dot_general(left, right, (((1,), (1,)), ((), ())), preferred_element_...  29.2 us
    all_to_all x1, blocking collectives, body(): lax.all_to_all(buffer, 'expert', split_axis=0, concat_axis=0, tiled=True)  24.2 us
    psum x1, blocking collectives, body(): rank_projection, score = lax.psum((low_part, score_part), 'mp')  17 us
    dot_general x1, matrix products, body(): jnp.dot(backward_result, first_factor_shard, preferred_element_type=jnp.f...  7.34 us
  transfers between devices with their start and end apart: 3, of which 1 were waited for; matrix products, arithmetic and copies ran while one was open for 4% of the time, Pallas kernels for 0%

profile of v1, /device:TPU:0, one launch (start us, length us, event | category | flops | bytes accessed | tf_op | source)
XLA Modules:
  0.0 217.8 jit_solution(14026074263682737755)
XLA Ops:
  7.2 0.0 copy-start
  7.2 0.0 copy-start.3
  7.2 0.0 copy-start.4
  7.2 0.0 all-gather.2.cloned.1.call-start
  7.2 0.9 copy.31
  8.1 0.1 eq.86
  8.3 0.1 eq.82
  8.4 1.2 reduce-window.6
  9.7 0.2 slice_reduce_fusion
  9.9 0.2 reduce-window.9
  10.1 0.1 add_bitcast_fusion
  10.2 0.1 reduce_sum.48
  10.3 0.1 copy.33
  10.4 0.7 multiply_add_fusion.1
  11.1 0.0 copy-done
  11.1 0.6 convolution_convert_fusion
  11.7 24.2 %all_to_all.20 = bf16[4,128,1536]{2,1,0:T(8,128)(2,1)} all-to-all(bf16[4,128,1536]{2,1,0:T(8,128)(2,1)S(1)} %bitcast.111), channel_id=1, replica_groups=mesh['groups'=2,'expert'=4,'mp'=4] {'expert'}, dimensions={0} | all-to-all | bytes 3145728 | tf_op jit(solution)/shard_map/all_to_all | solution.py:61
  35.9 0.0 all-gather.2.cloned.1.call-update
  35.9 0.0 copy-done.3
  35.9 0.2 add_reduce_fusion
  36.1 0.6 copy.34
  36.7 3.2 %all-to-all-start = ((bf16[4,1,128]{2,1,0:T(2,128)(2,1)}), bf16[4,1,128]{2,1,0:T(2,128)(2,1)S(1)}, u32[]{:S(2)}, u32[]{:S(2)}) async-start(bf16[4,1,128]{2,1,0:T(2,128)(2,1)} %copy.34), calls=%async_computation | async-start | bytes 4096 | tf_op jit(solution)/shard_map/all_to_all | solution.py:62
  39.9 0.0 copy-done.4
  39.9 0.0 copy-start.2
  39.9 3.6 %fusion.22 = f32[512,16]{0,1:T(8,128)S(1)} fusion(bf16[1,512,2048]{2,1,0:T(8,128)(2,1)} %param.12, bf16[1,512,2048]{2,1,0:T(8,128)(2,1)} %param.11, bf16[1,16,2048]{2,1,0:T(8,128)(2,1)S(1)} %copy-done.4), kind=kOutput, calls=%fused_computation.33 | convolution fusion | flops 41943040 | bytes 4292608 | tf_op jit(solution)/shard_map/dot_general | solution.py:19
  43.5 0.0 all-to-all-done
  43.6 108.7 %all-gather.2.cloned.1.call-done = bf16[512,6144]{1,0:T(8,128)(2,1)} async-done(((bf16[512,1536]{1,0:T(8,128)(2,1)}), bf16[512,6144]{1,0:T(8,128)(2,1)}) %all-gather.2.cloned.1.call-update) | async-done | bytes 6291472 | tf_op jit(solution)/shard_map/all_gather | solution.py:66
  152.3 0.0 copy-done.2
  152.3 4.5 %convolution_convert_fusion.1 = bf16[512,16]{0,1:T(8,128)(2,1)S(1)} fusion(bf16[512,6144]{1,0:T(8,128)(2,1)} %all-gather.2.cloned.1.call-done, bf16[1,16,6144]{2,1,0:T(8,128)(2,1)S(1)} %copy-done.2), kind=kOutput, calls=%fused_computation.36 | convolution fusion | flops 100671488 | bytes 6504448 | tf_op jit(solution)/shard_map/dot_general | solution.py:19
  156.8 21.1 %fusion = f32[512,2048]{1,0:T(8,128)} fusion(bf16[512,6144]{1,0:T(8,128)(2,1)} %all-gather.2.cloned.1.call-done, bf16[1,2048,6144]{2,1,0:T(8,128)(2,1)} %param.13), kind=kOutput, calls=%fused_computation | convolution fusion | flops 12884901888 | bytes 35651584 | tf_op jit(solution)/shard_map/dot_general | solution.py:19
  177.9 0.0 copy-start.1
  177.9 7.3 %multiply_reduce_fusion = (f32[512]{0:T(512)S(1)}, bf16[512,2048]{1,0:T(8,128)(2,1)}, bf16[1,512,2048]{2,1,0:T(8,128)(2,1)}, bf16[1,512,2048]{2,1,0:T(8,128)(2,1)}) fusion(bf16[1,512,2048]{2,1,0:T(8,128)(2,1)} %param.12, bf16[1,512,2048]{2,1,0:T(8,128)(2,1)} %param.11, f32[512]{0:T(512)S(1)} %bitcast.112, f32[512,2048]{1,0:T(8,128)} %fusion, ...), kind=kOutput, calls=%fused_computation.24 | convolution fusion | flops 57671168 | bytes 14766080 | tf_op jit(solution)/shard_map/dot_general | solution.py:76
  185.2 17.0 %all-reduce = (f32[512,16]{0,1:T(8,128)S(1)}, f32[4,1,128]{2,1,0:T(1,128)}) all-reduce(f32[512,16]{0,1:T(8,128)S(1)} %fusion.22, f32[4,1,128]{2,1,0:T(1,128)S(1)} %bitcast.128), channel_id=1, replica_groups=mesh['groups'=2,'expert'=4,'mp'=4] {'mp'}, use_global_device_ids=true, to_apply=%region_4.5 | all-reduce | flops 8704 | bytes 69632 | tf_op jit(solution)/shard_map/psum | solution.py:81
  202.3 3.2 %all-to-all-start.2 = ((f32[4,1,128]{2,1,0:T(1,128)}), f32[4,1,128]{2,1,0:T(1,128)S(1)}, u32[]{:S(2)}, u32[]{:S(2)}) async-start(f32[4,1,128]{2,1,0:T(1,128)} %get-tuple-element.8), calls=%async_computation.2 | async-start | bytes 4096 | tf_op jit(solution)/shard_map/all_to_all | solution.py:96
  205.5 3.2 %fusion.20 = f32[1,16,2048]{2,1,0:T(8,128)} fusion(bf16[512,2048]{1,0:T(8,128)(2,1)} %get-tuple-element.10, bf16[512,16]{0,1:T(8,128)(2,1)S(1)} %convolution_convert_fusion.1, f32[512]{0:T(512)S(1)} %bitcast.113), kind=kOutput, calls=%fused_computation.31 | convolution fusion | flops 201375744 | bytes 2246656 | tf_op jit(solution)/shard_map/dot_general | solution.py:86
  208.7 0.0 copy-done.1
  208.7 1.4 fusion.19
  210.1 0.0 all-to-all-done.2
  210.1 0.3 select_reduce_fusion.1
  210.3 0.6 pad_maximum_fusion
  (5 shorter events, 0.0 us)
Async XLA Ops:
  7.2 3.9 %copy-start = (bf16[256,1536]{1,0:T(8,128)(2,1)S(1)}, bf16[256,1536]{1,0:T(8,128)(2,1)}, u32[]{:S(2)}) copy-start(bf16[256,1536]{1,0:T(8,128)(2,1)} %param.8) | copy-start | bytes 2359300
  7.2 28.7 %copy-start.3 = (bf16[256,2]{0,1:T(2,128)(2,1)S(1)}, bf16[256,2]{0,1:T(2,128)(2,1)}, u32[]{:S(2)}) copy-start(bf16[256,2]{0,1:T(2,128)(2,1)} %param.10) | copy-start | bytes 3076
  7.2 32.7 %copy-start.4 = (bf16[1,16,2048]{2,1,0:T(8,128)(2,1)S(1)}, bf16[1,16,2048]{2,1,0:T(8,128)(2,1)}, u32[]{:S(2)}) copy-start(bf16[1,16,2048]{2,1,0:T(8,128)(2,1)} %param.14) | copy-start | bytes 196612
  7.2 145.1 %all-gather.2.cloned.1.call-start = ((), (), s32[]{:S(2)}) async-start(), calls=%async_computation.3 | async-start | bytes 7864320 | tf_op jit(solution)/shard_map/all_gather | solution.py:66
  36.7 6.9 %all-to-all-start = ((bf16[4,1,128]{2,1,0:T(2,128)(2,1)}), bf16[4,1,128]{2,1,0:T(2,128)(2,1)S(1)}, u32[]{:S(2)}, u32[]{:S(2)}) async-start(bf16[4,1,128]{2,1,0:T(2,128)(2,1)} %copy.34), calls=%async_computation | async-start | bytes 4096 | tf_op jit(solution)/shard_map/all_to_all | solution.py:62
  39.9 112.4 %copy-start.2 = (bf16[1,16,6144]{2,1,0:T(8,128)(2,1)S(1)}, bf16[1,16,6144]{2,1,0:T(8,128)(2,1)}, u32[]{:S(2)}) copy-start(bf16[1,16,6144]{2,1,0:T(8,128)(2,1)} %param.15) | copy-start | bytes 589828
  177.9 30.8 %copy-start.1 = (bf16[4,128,1536]{2,1,0:T(8,128)(2,1)S(1)}, bf16[4,128,1536]{2,1,0:T(8,128)(2,1)}, u32[]{:S(2)}) copy-start(bf16[4,128,1536]{2,1,0:T(8,128)(2,1)} %all_to_all.20) | copy-start | bytes 4718596
  202.3 7.8 %all-to-all-start.2 = ((f32[4,1,128]{2,1,0:T(1,128)}), f32[4,1,128]{2,1,0:T(1,128)S(1)}, u32[]{:S(2)}, u32[]{:S(2)}) async-start(f32[4,1,128]{2,1,0:T(1,128)} %get-tuple-element.8), calls=%async_computation.2 | async-start | bytes 4096 | tf_op jit(solution)/shard_map/all_to_all | solution.py:96
Sparse Core Ops, SparseCore 0:
  36.0 116.2 all-gather.1

commit v2 on v0

v2 whole, which is shorter than its diff:
```python
import functools

import jax
import jax.numpy as jnp
from jax import lax
from jax.experimental import pallas as pl
from jax.experimental.pallas import tpu as pltpu
from jax.sharding import PartitionSpec as P

CAP = 128
TILE = 256
LAG = 2
WBUFS = 4
MESH = pl.DeviceIdType.MESH

adapter_scale = 2.0


def positions(flat, count):
    hot = (flat[:, None] == jnp.arange(count, dtype=jnp.int32)[None, :]).astype(jnp.int32)
    before = jnp.cumsum(hot, axis=0) - hot
    return jnp.sum(before * hot, axis=1)


def contract_last(left, right):
    return lax.dot_general(
        left, right, (((1,), (1,)), ((), ())), preferred_element_type=jnp.float32
    )


def split_dot(left, right):
    high = left.astype(jnp.bfloat16)
    low = (left - high.astype(jnp.float32)).astype(jnp.bfloat16)
    return jnp.dot(high, right, preferred_element_type=jnp.float32) + jnp.dot(
        low, right, preferred_element_type=jnp.float32
    )


def turned(row, count):
    return jnp.transpose(jnp.broadcast_to(row, (count, row.shape[1])))


def kernel(
    n_z, n_e, halves,
    tok, meta, gate, up, weight, left_m, right_m,
    gate_out, up_out, a_out, b_out, w_out,
    tbuf, wbuf, dh, hid, coef, act, gbuf, ubuf, rows, own_rows, dmat, metas,
    pick_col, pick_row, back_t, low_acc, low_all, score_all, score_back, score_acc,
    load_sem, w_sem, io_sem, out_sem, zrecv, zright, zleft, xsend, xrecv, ssend, srecv,
    msend, mrecv, lsend, lrecv, csend, crecv, dsend, drecv,
):
    me = lax.axis_index("expert")
    z = lax.axis_index("mp")
    n_x = n_e // 2
    x, core = me // 2, me % 2
    width = tok.shape[1] // halves
    items = n_z * halves
    hidden_units = gate.shape[1]
    tiles = hidden_units // TILE

    def remote(src, dst, send, recv, where):
        return pltpu.make_async_remote_copy(
            src_ref=src, dst_ref=dst, send_sem=send, recv_sem=recv,
            device_id=where, device_id_type=MESH,
        )

    def zcopy(chunk, to, send):
        block = tbuf.at[chunk, me]
        return remote(block, block, send.at[chunk], zrecv.at[chunk], {"mp": to})

    def xcopy(chunk, k):
        block = tbuf.at[chunk, me]
        to = ((x + k) % n_x) * 2 + core
        return remote(block, block, xsend.at[k - 1, chunk], xrecv.at[k - 1, chunk], {"expert": to})

    def xarrival(chunk, k):
        block = tbuf.at[chunk, ((x + n_x - k) % n_x) * 2 + core]
        to = ((x + k) % n_x) * 2 + core
        return remote(block, block, xsend.at[k - 1, chunk], xrecv.at[k - 1, chunk], {"expert": to})

    def scopy(chunk, xs):
        block = tbuf.at[chunk, xs * 2 + core]
        return remote(block, block, ssend.at[xs, chunk], srecv.at[xs, chunk], {"expert": x * 2 + 1 - core})

    def sarrival(chunk, xs):
        block = tbuf.at[chunk, xs * 2 + 1 - core]
        return remote(block, block, ssend.at[xs, chunk], srecv.at[xs, chunk], {"expert": x * 2 + 1 - core})

    def spread(chunk):
        for k in range(1, n_x):
            xcopy(chunk, k).start()
        scopy(chunk, x).start()

    def item_chunk(i):
        j, h = i // halves, i % halves
        m = jnp.minimum(z, n_z - 1 - z)
        near = jnp.where(j % 2 == 1, z - (j + 1) // 2, z + j // 2)
        far = jnp.where(z > n_z - 1 - z, z - (j - m), z + (j - m))
        return jnp.where(j <= 2 * m, near, far) * halves + h

    def load(h):
        return pltpu.make_async_copy(
            tok.at[:, pl.ds(h * width, width)], tbuf.at[z * halves + h, me], load_sem.at[h]
        )

    def wload(i):
        chunk = item_chunk(i)
        return pltpu.make_async_copy(
            weight.at[:, pl.ds(pl.multiple_of(chunk * width, 128), width)],
            wbuf.at[i % WBUFS],
            w_sem.at[i % WBUFS],
        )

    for h in range(halves):
        load(h).start()
    gate_in = pltpu.make_async_copy(gate, gbuf, io_sem.at[0])
    up_in = pltpu.make_async_copy(up, ubuf, io_sem.at[1])
    gate_in.start()
    up_in.start()

    barrier = pltpu.get_barrier_semaphore()
    for k in range(1, n_e):
        pl.semaphore_signal(barrier, inc=1, device_id={"expert": (me + k) % n_e}, device_id_type=MESH)
    for k in range(1, n_z):
        pl.semaphore_signal(barrier, inc=1, device_id={"mp": (z + k) % n_z}, device_id_type=MESH)
    pl.semaphore_wait(barrier, n_e + n_z - 2)

    def mcopy(k):
        return remote(meta, metas.at[me], msend.at[k - 1], mrecv.at[k - 1], {"expert": (me + k) % n_e})

    def marrival(k):
        return remote(
            meta, metas.at[(me + n_e - k) % n_e], msend.at[k - 1], mrecv.at[k - 1],
            {"expert": (me + k) % n_e},
        )

    for k in range(1, n_e):
        mcopy(k).start()
    for h in range(halves):
        chunk = z * halves + h
        load(h).wait()

        @pl.when(z < n_z - 1)
        def _():
            zcopy(chunk, z + 1, zright).start()

        @pl.when(z > 0)
        def _():
            zcopy(chunk, z - 1, zleft).start()

        spread(chunk)
    for i in range(WBUFS):
        wload(i).start()
    metas[pl.ds(me, 1)] = meta[...][None]
    low_acc[...] = jnp.zeros_like(low_acc)
    back_t[...] = jnp.zeros_like(back_t)
    for k in range(1, n_e):
        marrival(k).wait_recv()
    tokens = meta.shape[1]
    slot = lax.broadcasted_iota(jnp.int32, (CAP, tokens), 0)

    def masks(keys, base):
        numbers = (slot + base).astype(jnp.float32)
        return numbers == keys[0:1, :], numbers == keys[1:2, :]

    for o in range(n_e):
        keys = metas[o]
        first, second = masks(keys, me * CAP)
        dmat[o] = (jnp.where(first, 1.0, 0.0) + jnp.where(second, 1.0, 0.0)).astype(jnp.bfloat16)
        col = jnp.sum(
            jnp.where(first, keys[2:3, :], 0.0) + jnp.where(second, keys[3:4, :], 0.0),
            axis=1, keepdims=True,
        )
        wide = jnp.broadcast_to(col, (CAP, 128))
        pick_col[o * CAP:(o + 1) * CAP, :] = wide
        pick_row[:, o * CAP:(o + 1) * CAP] = jnp.transpose(wide)[0:8, :]
    gate_in.wait()
    up_in.wait()

    def lcopy(k):
        return remote(low_acc, low_all.at[z], lsend.at[k - 1], lrecv.at[k - 1], {"mp": (z + k) % n_z})

    def larrival(k):
        return remote(
            low_acc, low_all.at[(z + n_z - k) % n_z], lsend.at[k - 1], lrecv.at[k - 1],
            {"mp": (z + k) % n_z},
        )

    def prepare(n):
        cols = pl.ds(pl.multiple_of(n * TILE, TILE), TILE)
        g = gbuf[:, cols].astype(jnp.float32)
        u = ubuf[:, cols].astype(jnp.float32)
        sigma = jax.nn.sigmoid(g)
        a = g * sigma
        hidden = (a * u).astype(jnp.bfloat16)
        hid[:, cols] = hidden
        act[:, cols] = a
        coef[:, cols] = u * sigma * (1.0 + g * (1.0 - sigma))
        dh[:, cols] = jnp.zeros((dh.shape[0], TILE), jnp.float32)
        low_acc[...] += contract_last(left_m[:, cols], hidden)

    per_step = -(-tiles // LAG)

    def product(i):
        chunk = item_chunk(i)
        for k in range(1, n_x):
            xarrival(chunk, k).wait_recv()
            scopy(chunk, (x + n_x - k) % n_x).start()
        for k in range(n_x):
            sarrival(chunk, (x + n_x - k) % n_x).wait_recv()
        for o in range(n_e):
            rows[o * CAP:(o + 1) * CAP, :] = jnp.dot(
                dmat[o], tbuf[chunk, o], preferred_element_type=jnp.float32
            ).astype(jnp.bfloat16)

        @pl.when(i < halves)
        def _():
            own_rows[i % halves] = rows[...]

        back_t[...] += contract_last(
            right_m[:, pl.ds(pl.multiple_of(chunk * width, 128), width)], rows[...]
        )
        wload(i).wait()

        def tile(n, carry):
            at = pl.ds(pl.multiple_of(n * TILE, TILE), TILE)
            dh[:, at] += contract_last(rows[...], wbuf[i % WBUFS, at, :])
            return carry

        lax.fori_loop(0, tiles, tile, 0)

        @pl.when(i + WBUFS < items)
        def _():
            wload(i + WBUFS).start()

    def step(t, carry):
        @pl.when((t >= halves) & (t < items))
        def _():
            d, h = t // halves, t % halves

            @pl.when(z - d >= 0)
            def _():
                chunk = (z - d) * halves + h
                zcopy(chunk, z, zright).wait_recv()

                @pl.when(z < n_z - 1)
                def _():
                    zcopy(chunk, z + 1, zright).start()

                spread(chunk)

            @pl.when(z + d < n_z)
            def _():
                chunk = (z + d) * halves + h
                zcopy(chunk, z, zleft).wait_recv()

                @pl.when(z > 0)
                def _():
                    zcopy(chunk, z - 1, zleft).start()

                spread(chunk)

        @pl.when(t < LAG)
        def _():
            def some(n, carry):
                prepare(n)
                return carry

            lax.fori_loop(t * per_step, jnp.minimum((t + 1) * per_step, tiles), some, 0)

        @pl.when(t >= LAG)
        def _():
            product(t - LAG)

        return carry

    lax.fori_loop(0, LAG, step, 0)
    low_all[pl.ds(z, 1)] = low_acc[...][None]
    for k in range(1, n_z):
        lcopy(k).start()
    lax.fori_loop(LAG, items + LAG, step, 0)

    back = back_t[...].astype(jnp.bfloat16).astype(jnp.float32)
    back_col = jnp.transpose(back).astype(jnp.bfloat16)
    score_acc[...] = jnp.zeros_like(score_acc)

    def outs(n):
        cols = pl.ds(pl.multiple_of(n * TILE, TILE), TILE)
        return (
            pltpu.make_async_copy(gbuf.at[:, cols], gate_out.at[:, cols], out_sem.at[0, n]),
            pltpu.make_async_copy(ubuf.at[:, cols], up_out.at[:, cols], out_sem.at[1, n]),
        )

    def finish(n, carry):
        cols = pl.ds(pl.multiple_of(n * TILE, TILE), TILE)
        d = dh[:, cols] + adapter_scale * jnp.dot(
            back_col, left_m[:, cols], preferred_element_type=jnp.float32
        )
        prod = hid[:, cols].astype(jnp.float32) * d
        total = prod[:, 0:128]
        for q in range(1, TILE // 128):
            total = total + prod[:, q * 128:(q + 1) * 128]
        score_acc[...] += total
        scaled = pick_col[:, 0:1] * d
        gbuf[:, cols] = (scaled * coef[:, cols]).astype(jnp.bfloat16)
        ubuf[:, cols] = (scaled * act[:, cols]).astype(jnp.bfloat16)
        for copy in outs(n):
            copy.start()
        return carry

    lax.fori_loop(0, tiles, finish, 0)

    mine = jnp.sum(jnp.transpose(score_acc[...]), axis=0, keepdims=True)
    score_all[pl.ds(z, 1)] = jnp.broadcast_to(mine, (8, mine.shape[1]))[None]

    def ccopy(k):
        block = score_all.at[z]
        return remote(block, block, csend.at[k - 1], crecv.at[k - 1], {"mp": (z + k) % n_z})

    def carrival(k):
        block = score_all.at[(z + n_z - k) % n_z]
        return remote(block, block, csend.at[k - 1], crecv.at[k - 1], {"mp": (z + k) % n_z})

    for k in range(1, n_z):
        ccopy(k).start()

    a_out[...] = adapter_scale * split_dot(pick_row[0:1, :] * back, hid[...])

    for k in range(1, n_z):
        carrival(k).wait_recv()
    whole = score_all[0]
    for k in range(1, n_z):
        whole = whole + score_all[k]
    for o in range(n_e):
        score_back[0, o] = whole[:, o * CAP:(o + 1) * CAP]

    def dcopy(k):
        to = (me + k) % n_e
        return remote(
            score_back.at[0, to], score_back.at[1, me], dsend.at[k - 1], drecv.at[k - 1], {"expert": to}
        )

    def darrival(k):
        return remote(
            score_back.at[0, (me + k) % n_e], score_back.at[1, (me + n_e - k) % n_e],
            dsend.at[k - 1], drecv.at[k - 1], {"expert": (me + k) % n_e},
        )

    for k in range(1, n_e):
        dcopy(k).start()
    score_back[1, pl.ds(me, 1)] = score_back[0, pl.ds(me, 1)]

    for k in range(1, n_z):
        larrival(k).wait_recv()
    low = low_all[0]
    for k in range(1, n_z):
        low = low + low_all[k]
    low = pick_row[0:1, :] * low
    for h in range(halves):
        b_out[:, h * width:(h + 1) * width] = adapter_scale * split_dot(low, own_rows[h])

    for k in range(1, n_e):
        darrival(k).wait_recv()
    firsts = jnp.zeros((1, tokens), jnp.float32)
    seconds = jnp.zeros((1, tokens), jnp.float32)
    for o in range(n_e):
        first, second = masks(meta[...], o * CAP)
        col = turned(score_back[1, o][0:1, :], CAP)[:, 0:1]
        firsts = firsts + jnp.sum(jnp.where(first, col, 0.0), axis=0, keepdims=True)
        seconds = seconds + jnp.sum(jnp.where(second, col, 0.0), axis=0, keepdims=True)
    w_out[0:1, :] = firsts
    w_out[1:2, :] = seconds

    def drain(chunk, carry):
        zs = chunk // halves

        @pl.when((zs <= z) & (z < n_z - 1))
        def _():
            zcopy(chunk, z + 1, zright).wait_send()

        @pl.when((zs >= z) & (z > 0))
        def _():
            zcopy(chunk, z - 1, zleft).wait_send()

        for k in range(1, n_x):
            xcopy(chunk, k).wait_send()
        for k in range(n_x):
            scopy(chunk, (x + k) % n_x).wait_send()
        return carry

    lax.fori_loop(0, items, drain, 0)
    for k in range(1, n_e):
        mcopy(k).wait_send()
        dcopy(k).wait_send()
    for k in range(1, n_z):
        lcopy(k).wait_send()
        ccopy(k).wait_send()

    def flush(n, carry):
        for copy in outs(n):
            copy.wait()
        return carry

    lax.fori_loop(0, tiles, flush, 0)


def body(
    output_gradient,
    routes,
    mixture_coefficients,
    gate_preactivation,
    up_projection_saved,
    down_matrix,
    lowrank_left_matrix,
    lowrank_right_matrix,
):
    n_e = lax.axis_size("expert")
    n_z = lax.axis_size("mp")
    tokens, span = output_gradient.shape
    halves = 2 if span % 256 == 0 else 1
    width = span // halves
    items = n_z * halves
    n_x = n_e // 2
    slots, units = gate_preactivation.shape[1:]
    rank = lowrank_left_matrix.shape[1]
    model = down_matrix.shape[2]
    tiles = units // TILE

    flat = routes.reshape(-1)
    key = (flat * CAP + positions(flat, n_e)).reshape(tokens, 2)
    meta = jnp.concatenate(
        [key.astype(jnp.float32).T, mixture_coefficients.astype(jnp.float32).T,
         jnp.zeros((4, tokens), jnp.float32)], axis=0
    )
    bf, f32 = jnp.bfloat16, jnp.float32
    anywhere = pl.BlockSpec(memory_space=pl.ANY)
    vmem = pl.BlockSpec(memory_space=pltpu.VMEM)
    dma = pltpu.SemaphoreType.DMA
    gate_grad, up_grad, a_grad, b_grad, scores = pl.pallas_call(
        functools.partial(kernel, n_z, n_e, halves),
        out_shape=(
            jax.ShapeDtypeStruct((slots, units), bf),
            jax.ShapeDtypeStruct((slots, units), bf),
            jax.ShapeDtypeStruct((rank, units), f32),
            jax.ShapeDtypeStruct((rank, span), f32),
            jax.ShapeDtypeStruct((2, tokens), f32),
        ),
        in_specs=[anywhere, vmem, anywhere, anywhere, anywhere, vmem, vmem],
        out_specs=(anywhere, anywhere, vmem, vmem, vmem),
        scratch_shapes=[
            pltpu.VMEM((items, n_e, tokens, width), bf),
            pltpu.VMEM((WBUFS, units, width), bf),
            pltpu.VMEM((slots, units), f32),
            pltpu.VMEM((slots, units), bf),
            pltpu.VMEM((slots, units), f32),
            pltpu.VMEM((slots, units), f32),
            pltpu.VMEM((slots, units), bf),
            pltpu.VMEM((slots, units), bf),
            pltpu.VMEM((slots, width), bf),
            pltpu.VMEM((halves, slots, width), bf),
            pltpu.VMEM((n_e, CAP, tokens), bf),
            pltpu.VMEM((n_e, 8, tokens), f32),
            pltpu.VMEM((slots, 128), f32),
            pltpu.VMEM((8, slots), f32),
            pltpu.VMEM((rank, slots), f32),
            pltpu.VMEM((rank, slots), f32),
            pltpu.VMEM((n_z, rank, slots), f32),
            pltpu.VMEM((n_z, 8, slots), f32),
            pltpu.VMEM((2, n_e, 8, CAP), f32),
            pltpu.VMEM((slots, 128), f32),
            dma((halves,)),
            dma((WBUFS,)),
            dma((2,)),
            dma((2, tiles)),
            dma((items,)),
            dma((items,)),
            dma((items,)),
            dma((n_x - 1, items)),
            dma((n_x - 1, items)),
            dma((n_x, items)),
            dma((n_x, items)),
            dma((n_e - 1,)),
            dma((n_e - 1,)),
            dma((n_z - 1,)),
            dma((n_z - 1,)),
            dma((n_z - 1,)),
            dma((n_z - 1,)),
            dma((n_e - 1,)),
            dma((n_e - 1,)),
        ],
        compiler_params=pltpu.CompilerParams(
            collective_id=0, has_side_effects=True, vmem_limit_bytes=60 * 1024 * 1024
        ),
        cost_estimate=pl.CostEstimate(
            flops=2 * slots * units * model,
            bytes_accessed=2 * units * model,
            transcendentals=slots * units,
        ),
    )(
        output_gradient, meta, gate_preactivation[0], up_projection_saved[0],
        down_matrix[0], lowrank_left_matrix[0], lowrank_right_matrix[0],
    )
    return gate_grad[None], up_grad[None], a_grad[None], b_grad[None], scores.T


def solution(mesh):
    placed = (
        P(("groups", "expert"), "mp"),
        P(("groups", "expert"), None),
        P(("groups", "expert"), None),
        P("expert", "groups", "mp"),
        P("expert", "groups", "mp"),
        P("expert", "mp", None),
        P("expert", None, "mp"),
        P("expert", None, None),
    )
    return jax.shard_map(
        body,
        mesh=mesh,
        in_specs=placed,
        out_specs=(
            P("expert", "groups", "mp"),
            P("expert", "groups", "mp"),
            P(("groups", "expert"), None, "mp"),
            P(("groups", "expert"), None, "mp"),
            P(("groups", "expert"), None),
        ),
        check_vma=False,
    )
```

time: 264 us -> 104 us (0.39)
  Pallas kernels: 0 us -> 91.8 us
  waiting for transfers between devices: 87.8 us -> 0 us
  local copies, waits for them, and re-layouts: 73 us -> 8.12 us
  blocking collectives: 41.4 us -> 0 us
  matrix products: 39.1 us -> 0 us
  between operations: 14.2 us -> 0.7 us
  starting transfers between devices: 6.66 us -> 0 us
    pallas_call x0 -> x1, Pallas kernels: none -> 91.8 us  [body(): pl.pallas_call(functools.partial(kernel, n_z, n_e, halves), out_shape=(ja...]
    all_gather x1 -> x0, waiting for transfers between devices: 85.5 us -> none  [body(): piece = lax.all_gather(slice_rows, 'mp', axis=1, tiled=True)]
    scatter x2 -> x0, local copies, waits for them, and re-layouts: 62.5 us -> none  [the longest x1 39.5 us: body(): jnp.zeros((experts, CAP, slice_width), jnp.bfloat16).at[flat, place]]
    dot_general x6 -> x0, matrix products: 39.1 us -> none  [the longest x3 29.2 us: contract_last(): lax.dot_general(left, right, (((1,), (1,)), ((), ())), preferred_element_...]
    all_to_all x1 -> x0, blocking collectives: 24.3 us -> none  [body(): lax.all_to_all(buffer, 'expert', split_axis=0, concat_axis=0, tiled=True)]
    psum x1 -> x0, blocking collectives: 17 us -> none  [body(): rank_projection, score = lax.psum((low_part, score_part), 'mp')]
    all_to_all x2 -> x0, starting transfers between devices: 6.63 us -> none  [the longest x1 3.4 us: body(): lax.all_to_all(owner_pick, 'expert', split_axis=0, concat_axis=0, tiled=T...]
    unnamed x11 -> x14, local copies, waits for them, and re-layouts: 1.68 us -> 7.33 us
  transfers between devices with their start and end apart: 3 -> 0, of which waited for: 2 -> 0; matrix products, arithmetic and copies ran while one was open for 11% -> 0% of each run, Pallas kernels for 0% -> 0%
where the time goes in v2:
time: 104 us
  Pallas kernels  91.8 us (88%)
  local copies, waits for them, and re-layouts  8.12 us (8%)
  other arithmetic  3.56 us (3%)
    pallas_call x1, Pallas kernels, body(): pl.pallas_call(functools.partial(kernel, n_z, n_e, halves), out_shape=(ja...  91.8 us
    unnamed x14, local copies, waits for them, and re-layouts  7.33 us

profile of v2, /device:TPU:0, one launch (start us, length us, event | category | flops | bytes accessed | tf_op | source)
XLA Modules:
  0.0 104.1 jit_solution(15744259489185850403)
XLA Ops:
  0.6 0.1 pad.2.clone
  0.7 0.7 convert_bitcast_fusion
  1.4 0.8 copy.13
  2.2 0.1 eq.29
  2.4 0.1 eq.25
  2.5 1.2 %reduce-window.6 = s32[4,4,128]{2,1,0:T(4,128)S(1)} reduce-window(s32[4,4,128]{2,1,0:T(4,128)S(1)} %fusion.3, s32[]{:T(128)} %constant.8.clone.1), window={size=1x1x128 pad=0_0x0_0x127_0}, to_apply=%region_0.0 | reduce-window | flops 260096 | bytes 16388 | tf_op jit(solution)/shard_map/reduce-window
  3.7 0.2 slice_reduce_fusion
  4.0 0.2 reduce-window.9
  4.1 0.1 add_bitcast_fusion
  4.2 0.1 reduce_sum.12
  4.4 0.1 copy.15
  4.5 0.7 convert_bitcast_fusion.1
  5.2 0.7 maximum_maximum_fusion.meta
  5.8 91.8 %shard_map.119 = (bf16[512,2048]{1,0:T(8,128)(2,1)}, bf16[512,2048]{1,0:T(8,128)(2,1)}, f32[16,2048]{1,0:T(8,128)}, f32[16,1536]{1,0:T(8,128)}, f32[2,256]{1,0:T(2,128)}) custom-call(bf16[256,1536]{1,0:T(8,128)(2,1)} %tok.1, f32[8,256]{1,0:T(8,128)} %maximum_maximum_fusion.meta, bf16[512,2048]{1,0:T(8,128)(2,1)} %bitcast.40, bf16[512,2048]{1,0:T(8,128)(2,1)} %bitcast.41, ...), custom_call_target="tpu_custom_call" | custom-call | flops 12884901888 | bytes 25165824 | tf_op jit(solution)/shard_map/pallas_call | solution.py:439
  97.6 0.0 copy-start
  97.6 3.3 %copy.23 = bf16[1,512,2048]{2,1,0:T(8,128)(2,1)} copy(bf16[1,512,2048]{2,1,0:T(8,128)(2,1)} %bitcast.34) | data formatting | bytes 4194304
  100.9 0.0 copy-done
  100.9 0.0 copy-start.1
  100.9 0.0 copy-start.2
  100.9 0.0 copy-start.3
  100.9 1.3 %copy.24 = bf16[1,512,2048]{2,1,0:T(8,128)(2,1)} copy(bf16[1,512,2048]{2,1,0:T(8,128)(2,1)S(1)} %bitcast.33) | data formatting | bytes 4194304
  102.3 0.0 copy-done.1
  102.3 0.7 copy.25
  102.9 0.0 copy-done.2
  102.9 0.6 copy.26
  103.6 0.0 copy-done.3
  103.6 0.6 copy.27
  (3 shorter events, 0.0 us)
Async XLA Ops:
  97.6 3.3 %copy-start = (bf16[512,2048]{1,0:T(8,128)(2,1)S(1)}, bf16[512,2048]{1,0:T(8,128)(2,1)}, u32[]{:S(2)}) copy-start(bf16[512,2048]{1,0:T(8,128)(2,1)} %get-tuple-element.11) | copy-start | bytes 6291460
  100.9 1.3 %copy-start.1 = (f32[16,2048]{1,0:T(8,128)S(1)}, f32[16,2048]{1,0:T(8,128)}, u32[]{:S(2)}) copy-start(f32[16,2048]{1,0:T(8,128)} %get-tuple-element.12) | copy-start | bytes 393220
  100.9 2.0 %copy-start.2 = (f32[16,1536]{1,0:T(8,128)S(1)}, f32[16,1536]{1,0:T(8,128)}, u32[]{:S(2)}) copy-start(f32[16,1536]{1,0:T(8,128)} %get-tuple-element.13) | copy-start | bytes 294916
  100.9 2.6 %copy-start.3 = (f32[2,256]{1,0:T(2,128)S(1)}, f32[2,256]{1,0:T(2,128)}, u32[]{:S(2)}) copy-start(f32[2,256]{1,0:T(2,128)} %get-tuple-element.14) | copy-start | bytes 6148

commit v3 on v2

--- a/solution.py
+++ b/solution.py
@@ -16,12 +16,6 @@
 adapter_scale = 2.0
 
 
-def positions(flat, count):
-    hot = (flat[:, None] == jnp.arange(count, dtype=jnp.int32)[None, :]).astype(jnp.int32)
-    before = jnp.cumsum(hot, axis=0) - hot
-    return jnp.sum(before * hot, axis=1)
-
-
 def contract_last(left, right):
     return lax.dot_general(
         left, right, (((1,), (1,)), ((), ())), preferred_element_type=jnp.float32
@@ -42,12 +36,12 @@
 
 def kernel(
     n_z, n_e, halves,
-    tok, meta, gate, up, weight, left_m, right_m,
+    tok, routes, mix, gate, up, weight, left_m, right_m,
     gate_out, up_out, a_out, b_out, w_out,
-    tbuf, wbuf, dh, hid, coef, act, gbuf, ubuf, rows, own_rows, dmat, metas,
+    tbuf, wbuf, dh, hid, coef, act, gbuf, ubuf, rows, own_rows, dmat, meta, metas,
     pick_col, pick_row, back_t, low_acc, low_all, score_all, score_back, score_acc,
     load_sem, w_sem, io_sem, out_sem, zrecv, zright, zleft, xsend, xrecv, ssend, srecv,
-    msend, mrecv, lsend, lrecv, csend, crecv, dsend, drecv,
+    psend, precv, msend, mrecv, lsend, lrecv, csend, crecv, dsend, drecv,
 ):
     me = lax.axis_index("expert")
     z = lax.axis_index("mp")
@@ -57,6 +51,9 @@
     items = n_z * halves
     hidden_units = gate.shape[1]
     tiles = hidden_units // TILE
+    detour = n_x == 2 and halves == 2 and n_z % 2 == 0
+    pair = z + 1 - 2 * (z % 2)
+    late_at = jnp.where((z % 2 == 1) | (z == 0), 3, 5)
 
     def remote(src, dst, send, recv, where):
         return pltpu.make_async_remote_copy(
@@ -86,12 +83,28 @@
         block = tbuf.at[chunk, xs * 2 + 1 - core]
         return remote(block, block, ssend.at[xs, chunk], srecv.at[xs, chunk], {"expert": x * 2 + 1 - core})
 
+    def direct(chunk):
+        return (chunk != pair * halves + 1) if detour else (chunk >= 0)
+
+    def pcopy():
+        block = tbuf.at[z * halves + 1, (1 - x) * 2 + core]
+        return remote(block, block, psend.at[0], precv.at[0], {"mp": pair})
+
+    def parrival():
+        block = tbuf.at[pair * halves + 1, (1 - x) * 2 + core]
+        return remote(block, block, psend.at[0], precv.at[0], {"mp": pair})
+
     def spread(chunk):
-        for k in range(1, n_x):
-            xcopy(chunk, k).start()
+        @pl.when(direct(chunk))
+        def _():
+            for k in range(1, n_x):
+                xcopy(chunk, k).start()
+
         scopy(chunk, x).start()
 
     def item_chunk(i):
+        if detour:
+            i = jnp.where(i < late_at, i, jnp.where(i == items - 1, late_at, i + 1))
         j, h = i // halves, i % halves
         m = jnp.minimum(z, n_z - 1 - z)
         near = jnp.where(j % 2 == 1, z - (j + 1) // 2, z + j // 2)
@@ -134,8 +147,6 @@
             {"expert": (me + k) % n_e},
         )
 
-    for k in range(1, n_e):
-        mcopy(k).start()
     for h in range(halves):
         chunk = z * halves + h
         load(h).wait()
@@ -151,12 +162,32 @@
         spread(chunk)
     for i in range(WBUFS):
         wload(i).start()
+    tokens = routes.shape[1]
+    named = routes[...].astype(jnp.float32)
+    wanted = lax.broadcasted_iota(jnp.int32, (16, tokens), 0).astype(jnp.float32)
+    hot = jnp.where(wanted == named[0:1, :], 1.0, 0.0) + jnp.where(wanted == named[1:2, :], 1.0, 0.0)
+    earlier = (
+        lax.broadcasted_iota(jnp.int32, (tokens, tokens), 0)
+        < lax.broadcasted_iota(jnp.int32, (tokens, tokens), 1)
+    )
+    before = jnp.dot(
+        hot.astype(jnp.bfloat16),
+        jnp.where(earlier, 1.0, 0.0).astype(jnp.bfloat16),
+        preferred_element_type=jnp.float32,
+    )
+    meta[...] = jnp.zeros_like(meta)
+    for k in range(2):
+        one = named[k:k + 1, :]
+        place = jnp.sum(jnp.where(wanted == one, before, 0.0), axis=0, keepdims=True)
+        meta[k:k + 1, :] = one * CAP + place
+    meta[2:4, :] = mix[...].astype(jnp.float32)
+    for k in range(1, n_e):
+        mcopy(k).start()
     metas[pl.ds(me, 1)] = meta[...][None]
     low_acc[...] = jnp.zeros_like(low_acc)
     back_t[...] = jnp.zeros_like(back_t)
     for k in range(1, n_e):
         marrival(k).wait_recv()
-    tokens = meta.shape[1]
     slot = lax.broadcasted_iota(jnp.int32, (CAP, tokens), 0)
 
     def masks(keys, base):
@@ -203,8 +234,17 @@
 
     def product(i):
         chunk = item_chunk(i)
+        @pl.when(direct(chunk))
+        def _():
+            for k in range(1, n_x):
+                xarrival(chunk, k).wait_recv()
+
+        if detour:
+            @pl.when(chunk == pair * halves + 1)
+            def _():
+                parrival().wait_recv()
+
         for k in range(1, n_x):
-            xarrival(chunk, k).wait_recv()
             scopy(chunk, (x + n_x - k) % n_x).start()
         for k in range(n_x):
             sarrival(chunk, (x + n_x - k) % n_x).wait_recv()
@@ -260,6 +300,11 @@
 
                 spread(chunk)
 
+        if detour:
+            @pl.when(t == items - halves - 1)
+            def _():
+                pcopy().start()
+
         @pl.when(t < LAG)
         def _():
             def some(n, carry):
@@ -281,7 +326,8 @@
     lax.fori_loop(LAG, items + LAG, step, 0)
 
     back = back_t[...].astype(jnp.bfloat16).astype(jnp.float32)
-    back_col = jnp.transpose(back).astype(jnp.bfloat16)
+    back_col = (adapter_scale * jnp.transpose(back)).astype(jnp.bfloat16)
+    pick = jnp.concatenate([pick_col[...]] * (TILE // 128), axis=1)
     score_acc[...] = jnp.zeros_like(score_acc)
 
     def outs(n):
@@ -293,7 +339,7 @@
 
     def finish(n, carry):
         cols = pl.ds(pl.multiple_of(n * TILE, TILE), TILE)
-        d = dh[:, cols] + adapter_scale * jnp.dot(
+        d = dh[:, cols] + jnp.dot(
             back_col, left_m[:, cols], preferred_element_type=jnp.float32
         )
         prod = hid[:, cols].astype(jnp.float32) * d
@@ -301,7 +347,7 @@
         for q in range(1, TILE // 128):
             total = total + prod[:, q * 128:(q + 1) * 128]
         score_acc[...] += total
-        scaled = pick_col[:, 0:1] * d
+        scaled = pick * d
         gbuf[:, cols] = (scaled * coef[:, cols]).astype(jnp.bfloat16)
         ubuf[:, cols] = (scaled * act[:, cols]).astype(jnp.bfloat16)
         for copy in outs(n):
@@ -382,13 +428,18 @@
         def _():
             zcopy(chunk, z - 1, zleft).wait_send()
 
-        for k in range(1, n_x):
-            xcopy(chunk, k).wait_send()
+        @pl.when(direct(chunk))
+        def _():
+            for k in range(1, n_x):
+                xcopy(chunk, k).wait_send()
+
         for k in range(n_x):
             scopy(chunk, (x + k) % n_x).wait_send()
         return carry
 
     lax.fori_loop(0, items, drain, 0)
+    if detour:
+        pcopy().wait_send()
     for k in range(1, n_e):
         mcopy(k).wait_send()
         dcopy(k).wait_send()
@@ -426,12 +477,6 @@
     model = down_matrix.shape[2]
     tiles = units // TILE
 
-    flat = routes.reshape(-1)
-    key = (flat * CAP + positions(flat, n_e)).reshape(tokens, 2)
-    meta = jnp.concatenate(
-        [key.astype(jnp.float32).T, mixture_coefficients.astype(jnp.float32).T,
-         jnp.zeros((4, tokens), jnp.float32)], axis=0
-    )
     bf, f32 = jnp.bfloat16, jnp.float32
     anywhere = pl.BlockSpec(memory_space=pl.ANY)
     vmem = pl.BlockSpec(memory_space=pltpu.VMEM)
@@ -445,7 +490,7 @@
             jax.ShapeDtypeStruct((rank, span), f32),
             jax.ShapeDtypeStruct((2, tokens), f32),
         ),
-        in_specs=[anywhere, vmem, anywhere, anywhere, anywhere, vmem, vmem],
+        in_specs=[anywhere, vmem, vmem, anywhere, anywhere, anywhere, vmem, vmem],
         out_specs=(anywhere, anywhere, vmem, vmem, vmem),
         scratch_shapes=[
             pltpu.VMEM((items, n_e, tokens, width), bf),
@@ -459,6 +504,7 @@
             pltpu.VMEM((slots, width), bf),
             pltpu.VMEM((halves, slots, width), bf),
             pltpu.VMEM((n_e, CAP, tokens), bf),
+            pltpu.VMEM((8, tokens), f32),
             pltpu.VMEM((n_e, 8, tokens), f32),
             pltpu.VMEM((slots, 128), f32),
             pltpu.VMEM((8, slots), f32),
@@ -479,6 +525,8 @@
             dma((n_x - 1, items)),
             dma((n_x, items)),
             dma((n_x, items)),
+            dma((1,)),
+            dma((1,)),
             dma((n_e - 1,)),
             dma((n_e - 1,)),
             dma((n_z - 1,)),
@@ -497,7 +545,7 @@
             transcendentals=slots * units,
         ),
     )(
-        output_gradient, meta, gate_preactivation[0], up_projection_saved[0],
+        output_gradient, routes.T, mixture_coefficients.T, gate_preactivation[0], up_projection_saved[0],
         down_matrix[0], lowrank_left_matrix[0], lowrank_right_matrix[0],
     )
     return gate_grad[None], up_grad[None], a_grad[None], b_grad[None], scores.T

time: 104 us -> 107 us (1.029)
  Pallas kernels: 91.8 us -> 99.3 us
  other arithmetic: 3.56 us -> 0 us
  local copies, waits for them, and re-layouts: 8.12 us -> 6.52 us
    pallas_call x1, Pallas kernels: 91.8 us -> 99.3 us  [body(): pl.pallas_call(functools.partial(kernel, n_z, n_e, halves), out_shape=(ja...]
    another operation x2 -> x0, other arithmetic: 1.41 us -> none
    transpose x2 -> x0, other arithmetic: 1.38 us -> none  [the longest x1 0.7 us: body(): key.astype(jnp.float32)]
    unnamed x14 -> x13, local copies, waits for them, and re-layouts: 7.33 us -> 6.52 us
where the time goes in v3:
time: 107 us; the launch traced here: 106 us
  Pallas kernels  99.3 us (93%)
  local copies, waits for them, and re-layouts  6.52 us (6%)
    pallas_call x1, Pallas kernels, body(): pl.pallas_call(functools.partial(kernel, n_z, n_e, halves), out_shape=(ja...  99.3 us
    unnamed x13, local copies, waits for them, and re-layouts  6.52 us

profile of v3, /device:TPU:0, one launch (start us, length us, event | category | flops | bytes accessed | tf_op | source)
XLA Modules:
  0.0 106.5 jit_solution(15165678596985743142)
XLA Ops:
  0.6 99.3 %shard_map.119 = (bf16[512,2048]{1,0:T(8,128)(2,1)}, bf16[512,2048]{1,0:T(8,128)(2,1)}, f32[16,2048]{1,0:T(8,128)}, f32[16,1536]{1,0:T(8,128)}, f32[2,256]{1,0:T(2,128)}) custom-call(bf16[256,1536]{1,0:T(8,128)(2,1)} %tok.1, s32[2,256]{1,0:T(2,128)} %bitcast.22, bf16[2,256]{1,0:T(2,128)(2,1)} %bitcast.23, bf16[512,2048]{1,0:T(8,128)(2,1)} %bitcast.18, ...), custom_call_target="tpu_custom_call" | custom-call | flops 12884901888 | bytes 25165824 | tf_op jit(solution)/shard_map/pallas_call | solution.py:484
  99.9 0.0 copy-start
  99.9 3.3 %copy.18 = bf16[1,512,2048]{2,1,0:T(8,128)(2,1)} copy(bf16[1,512,2048]{2,1,0:T(8,128)(2,1)} %bitcast.13) | data formatting | bytes 4194304
  103.2 0.0 copy-done
  103.2 0.0 copy-start.1
  103.2 0.0 copy-start.2
  103.2 0.0 copy-start.3
  103.2 1.3 %copy.19 = bf16[1,512,2048]{2,1,0:T(8,128)(2,1)} copy(bf16[1,512,2048]{2,1,0:T(8,128)(2,1)S(1)} %bitcast.12) | data formatting | bytes 4194304
  104.6 0.0 copy-done.1
  104.6 0.7 copy.20
  105.2 0.0 copy-done.2
  105.2 0.6 copy.21
  105.9 0.0 copy-done.3
  105.9 0.6 copy.22
Async XLA Ops:
  99.9 3.3 %copy-start = (bf16[512,2048]{1,0:T(8,128)(2,1)S(1)}, bf16[512,2048]{1,0:T(8,128)(2,1)}, u32[]{:S(2)}) copy-start(bf16[512,2048]{1,0:T(8,128)(2,1)} %get-tuple-element.11) | copy-start | bytes 6291460
  103.2 1.3 %copy-start.1 = (f32[16,2048]{1,0:T(8,128)S(1)}, f32[16,2048]{1,0:T(8,128)}, u32[]{:S(2)}) copy-start(f32[16,2048]{1,0:T(8,128)} %get-tuple-element.12) | copy-start | bytes 393220
  103.2 2.0 %copy-start.2 = (f32[16,1536]{1,0:T(8,128)S(1)}, f32[16,1536]{1,0:T(8,128)}, u32[]{:S(2)}) copy-start(f32[16,1536]{1,0:T(8,128)} %get-tuple-element.13) | copy-start | bytes 294916
  103.2 2.6 %copy-start.3 = (f32[2,256]{1,0:T(2,128)S(1)}, f32[2,256]{1,0:T(2,128)}, u32[]{:S(2)}) copy-start(f32[2,256]{1,0:T(2,128)} %get-tuple-element.14) | copy-start | bytes 6148

commit v4 on v3

--- a/solution.py
+++ b/solution.py
@@ -51,7 +51,8 @@
     items = n_z * halves
     hidden_units = gate.shape[1]
     tiles = hidden_units // TILE
-    detour = n_x == 2 and halves == 2 and n_z % 2 == 0
+    wide_tile = min(hidden_units, 1024)
+    detour = False
     pair = z + 1 - 2 * (z % 2)
     late_at = jnp.where((z % 2 == 1) | (z == 0), 3, 5)
 
@@ -258,20 +259,30 @@
             own_rows[i % halves] = rows[...]
 
         back_t[...] += contract_last(
-            right_m[:, pl.ds(pl.multiple_of(chunk * width, 128), width)], rows[...]
+            rows[...], right_m[:, pl.ds(pl.multiple_of(chunk * width, 128), width)]
         )
         wload(i).wait()
 
         def tile(n, carry):
-            at = pl.ds(pl.multiple_of(n * TILE, TILE), TILE)
+            at = pl.ds(pl.multiple_of(n * wide_tile, TILE), wide_tile)
             dh[:, at] += contract_last(rows[...], wbuf[i % WBUFS, at, :])
             return carry
 
-        lax.fori_loop(0, tiles, tile, 0)
+        lax.fori_loop(0, hidden_units // wide_tile, tile, 0)
 
         @pl.when(i + WBUFS < items)
         def _():
             wload(i + WBUFS).start()
+
+    def right_sums():
+        for k in range(1, n_z):
+            larrival(k).wait_recv()
+        low = low_all[0]
+        for k in range(1, n_z):
+            low = low + low_all[k]
+        low = pick_row[0:1, :] * low
+        for h in range(halves):
+            b_out[:, h * width:(h + 1) * width] = adapter_scale * split_dot(low, own_rows[h])
 
     def step(t, carry):
         @pl.when((t >= halves) & (t < items))
@@ -316,6 +327,10 @@
         @pl.when(t >= LAG)
         def _():
             product(t - LAG)
+
+        @pl.when(t == items - 1)
+        def _():
+            right_sums()
 
         return carry
 
@@ -325,8 +340,9 @@
         lcopy(k).start()
     lax.fori_loop(LAG, items + LAG, step, 0)
 
-    back = back_t[...].astype(jnp.bfloat16).astype(jnp.float32)
-    back_col = (adapter_scale * jnp.transpose(back)).astype(jnp.bfloat16)
+    rounded = back_t[...].astype(jnp.bfloat16).astype(jnp.float32)
+    back = jnp.transpose(rounded)
+    back_col = (adapter_scale * rounded).astype(jnp.bfloat16)
     pick = jnp.concatenate([pick_col[...]] * (TILE // 128), axis=1)
     score_acc[...] = jnp.zeros_like(score_acc)
 
@@ -395,15 +411,6 @@
     for k in range(1, n_e):
         dcopy(k).start()
     score_back[1, pl.ds(me, 1)] = score_back[0, pl.ds(me, 1)]
-
-    for k in range(1, n_z):
-        larrival(k).wait_recv()
-    low = low_all[0]
-    for k in range(1, n_z):
-        low = low + low_all[k]
-    low = pick_row[0:1, :] * low
-    for h in range(halves):
-        b_out[:, h * width:(h + 1) * width] = adapter_scale * split_dot(low, own_rows[h])
 
     for k in range(1, n_e):
         darrival(k).wait_recv()
@@ -508,7 +515,7 @@
             pltpu.VMEM((n_e, 8, tokens), f32),
             pltpu.VMEM((slots, 128), f32),
             pltpu.VMEM((8, slots), f32),
-            pltpu.VMEM((rank, slots), f32),
+            pltpu.VMEM((slots, rank), f32),
             pltpu.VMEM((rank, slots), f32),
             pltpu.VMEM((n_z, rank, slots), f32),
             pltpu.VMEM((n_z, 8, slots), f32),

time: 107 us -> 103 us (0.963)
  Pallas kernels: 99.3 us -> 95.8 us
    pallas_call x1, Pallas kernels: 99.3 us -> 95.8 us  [body(): pl.pallas_call(functools.partial(kernel, n_z, n_e, halves), out_shape=(ja...]
where the time goes in v4:
time: 103 us
  Pallas kernels  95.8 us (93%)
  local copies, waits for them, and re-layouts  6.52 us (6%)
    pallas_call x1, Pallas kernels, body(): pl.pallas_call(functools.partial(kernel, n_z, n_e, halves), out_shape=(ja...  95.8 us
    unnamed x13, local copies, waits for them, and re-layouts  6.52 us

profile of v4, /device:TPU:0, one launch (start us, length us, event | category | flops | bytes accessed | tf_op | source)
XLA Modules:
  0.0 103.0 jit_solution(11077602404841773191)
XLA Ops:
  0.6 95.8 %shard_map.119 = (bf16[512,2048]{1,0:T(8,128)(2,1)}, bf16[512,2048]{1,0:T(8,128)(2,1)}, f32[16,2048]{1,0:T(8,128)}, f32[16,1536]{1,0:T(8,128)}, f32[2,256]{1,0:T(2,128)}) custom-call(bf16[256,1536]{1,0:T(8,128)(2,1)} %tok.1, s32[2,256]{1,0:T(2,128)} %bitcast.22, bf16[2,256]{1,0:T(2,128)(2,1)} %bitcast.23, bf16[512,2048]{1,0:T(8,128)(2,1)} %bitcast.18, ...), custom_call_target="tpu_custom_call" | custom-call | flops 12884901888 | bytes 25165824 | tf_op jit(solution)/shard_map/pallas_call | solution.py:491
  96.5 0.0 copy-start
  96.5 3.3 %copy.18 = bf16[1,512,2048]{2,1,0:T(8,128)(2,1)} copy(bf16[1,512,2048]{2,1,0:T(8,128)(2,1)} %bitcast.13) | data formatting | bytes 4194304
  99.8 0.0 copy-done
  99.8 0.0 copy-start.1
  99.8 0.0 copy-start.2
  99.8 0.0 copy-start.3
  99.8 1.3 %copy.19 = bf16[1,512,2048]{2,1,0:T(8,128)(2,1)} copy(bf16[1,512,2048]{2,1,0:T(8,128)(2,1)S(1)} %bitcast.12) | data formatting | bytes 4194304
  101.1 0.0 copy-done.1
  101.1 0.7 copy.20
  101.8 0.0 copy-done.2
  101.8 0.6 copy.21
  102.4 0.0 copy-done.3
  102.4 0.6 copy.22
Async XLA Ops:
  96.5 3.3 %copy-start = (bf16[512,2048]{1,0:T(8,128)(2,1)S(1)}, bf16[512,2048]{1,0:T(8,128)(2,1)}, u32[]{:S(2)}) copy-start(bf16[512,2048]{1,0:T(8,128)(2,1)} %get-tuple-element.11) | copy-start | bytes 6291460
  99.8 1.3 %copy-start.1 = (f32[16,2048]{1,0:T(8,128)S(1)}, f32[16,2048]{1,0:T(8,128)}, u32[]{:S(2)}) copy-start(f32[16,2048]{1,0:T(8,128)} %get-tuple-element.12) | copy-start | bytes 393220
  99.8 2.0 %copy-start.2 = (f32[16,1536]{1,0:T(8,128)S(1)}, f32[16,1536]{1,0:T(8,128)}, u32[]{:S(2)}) copy-start(f32[16,1536]{1,0:T(8,128)} %get-tuple-element.13) | copy-start | bytes 294916
  99.8 2.6 %copy-start.3 = (f32[2,256]{1,0:T(2,128)S(1)}, f32[2,256]{1,0:T(2,128)}, u32[]{:S(2)}) copy-start(f32[2,256]{1,0:T(2,128)} %get-tuple-element.14) | copy-start | bytes 6148
